TPU v7x, 128 devices: a whole 4x4x4 slice. The times are simulated.
128 devices in a mesh: gx: 8 (over x, core), gy: 16 (over z, y).
Axes of the slice: x: 4, y: 4, z: 4, core: 2. Of those that a mesh axis runs over, the one named last changes fastest.
Arguments:
- sources: float32 [16, 4194304], P(None, ('gx', 'gy')), may hold values from -6 to 6
- leaf_basis: float32 [4096, 48, 1024], P(('gx', 'gy')), may hold values from -0.1875 to 0.1875
- level_blocks: float32 [8, 2, 48, 48, 4096], P(None, None, None, None, ('gx', 'gy')), may hold values from -0.625 to 0.625
- out_basis: float32 [4096, 48, 1024], P(('gx', 'gy')), may hold values from -0.875 to 0.875
Outputs:
- applied: float32 [16, 4194304], P(None, ('gx', 'gy'))
All inputs are finite; a program needn't handle non-finite values.
Results may differ from a plain program's by a relative error of at most 0.00011.
Values sent between devices are 32-bit elements; how exact they have to be, the bound alone decides.
A program may use at most 128 MiB of HBM per device.

v0:
```python
import jax
import jax.numpy as jnp
from jax import lax
from jax.sharding import PartitionSpec as P


def swapped(block, axis, bit):
    count = lax.axis_size(axis)
    route = []
    for low in range(count):
        high = low | 1 << bit
        if high != low and high < count:
            route += [(low, high), (high, low)]
    return lax.ppermute(block, axis, route)


def partner_of(state, stride):
    rank_n, count, total = state.shape
    view = state.reshape(rank_n, count, total // (2 * stride), 2, stride)
    return jnp.flip(view, 3).reshape(rank_n, count, total)


def combine(blocks, state, other):
    own_term = jnp.einsum("abg,bsg->asg", blocks[0], state, precision=lax.Precision.HIGHEST)
    far_term = jnp.einsum("abg,bsg->asg", blocks[1], other, precision=lax.Precision.HIGHEST)
    return own_term + far_term


def body(sources, leaf_basis, level_blocks, out_basis):
    boxes_here, rank_n, leaf_n = leaf_basis.shape
    count = sources.shape[0]
    points = sources.reshape(count, boxes_here, leaf_n)
    state = jnp.einsum("sgp,grp->rsg", points, leaf_basis, precision=lax.Precision.HIGHEST)
    xbits = lax.axis_size("gx").bit_length() - 1
    ybits = lax.axis_size("gy").bit_length() - 1
    levels_n = level_blocks.shape[0]
    local_n = levels_n - xbits - ybits
    plan = [("local", 0)]
    plan = plan + [("column", j) for j in range(ybits)]
    plan = plan + [("row", j) for j in range(xbits)]
    for level, (where, bit) in enumerate(plan):
        if where == "local":
            other = partner_of(state, 2**bit)
        elif where == "column":
            other = swapped(state, "gy", bit)
        else:
            other = swapped(state, "gx", bit)
        state = combine(level_blocks[level], state, other)
    moved = lax.all_to_all(state, "gy", split_axis=2, concat_axis=2, tiled=True)
    applied = jnp.einsum("grp,rsg->sgp", out_basis, moved, precision=lax.Precision.HIGHEST)
    return applied.reshape(count, boxes_here * leaf_n)


def solution(mesh):
    placed = (
        P(None, ("gx", "gy")),
        P(("gx", "gy"), None, None),
        P(None, None, None, None, ("gx", "gy")),
        P(("gx", "gy"), None, None),
    )
    return jax.shard_map(
        body, mesh=mesh, in_specs=placed, out_specs=P(None, ("gx", "gy")), check_vma=False
    )
```

profile of v0, /device:TPU:0, one launch (start us, length us, event | category | flops | bytes accessed | tf_op | source)
XLA Modules:
  0.0 112.3 jit_solution(6950310694983995424)
XLA Ops:
  0.0 0.0 copy-start
  0.0 9.6 %slice_bitcast_fusion = (f32[48,48,32]{1,2,0:T(8,128)}, f32[1,1,48,48,32]{3,4,2,1,0:T(8,128)}, f32[1,1,48,48,32]{3,4,2,1,0:T(8,128)}, f32[1,1,48,48,32]{3,4,2,1,...) fusion(f32[8,2,48,48,32]{3,4,2,1,0:T(8,128)} %param.6), kind=kLoop, calls=%fused_computation.44 | loop fusion | bytes 9437184 | tf_op jit(solution)/shard_map/squeeze | solution.py:25
  9.6 0.0 copy-start.12
  9.6 0.0 copy-done
  9.6 7.2 %fusion = f32[32,48,16]{1,2,0:T(8,128)S(1)} fusion(f32[32,48,1024]{2,1,0:T(8,128)S(1)} %copy-done, f32[2,32,8,1024]{3,2,1,0:T(8,128)} %bitcast.101), kind=kOutput, calls=%fused_computation | convolution fusion | flops 301989888 | bytes 8486912 | tf_op jit(solution)/shard_map/sgp,grp->rsg/dot_general | solution.py:33
  16.8 0.0 copy-start.10
  16.8 0.0 copy-start.9
  16.8 0.0 copy-start.8
  16.8 0.0 copy-done.12
  16.8 2.4 %fusion.17 = f32[32,16,48]{2,1,0:T(8,128)} fusion(f32[1,1,48,48,32]{3,4,2,1,0:T(8,128)S(1)} %copy-done.12, f32[32,48,16]{1,2,0:T(8,128)S(1)} %fusion), kind=kOutput, calls=%fused_computation.40 | convolution fusion | flops 14155776 | bytes 491520 | tf_op jit(solution)/shard_map/abg,bsg->asg/dot_general | solution.py:24
  19.2 0.0 copy-start.7
  19.2 0.7 rev.4
  19.9 0.0 copy-start.11
  19.9 0.0 copy-start.6
  19.9 3.1 %fusion.10 = f32[48,16,32]{0,1,2:T(8,128)S(1)} fusion(f32[32,16,48]{2,1,0:T(8,128)} %fusion.17, f32[48,16,32]{0,1,2:T(8,128)} %bitcast.102, f32[1,1,48,48,32]{3,4,2,1,0:T(8,128)} %get-tuple-element.17), kind=kOutput, calls=%fused_computation.19 | convolution fusion | flops 14180352 | bytes 589824 | tf_op jit(solution)/shard_map/abg,bsg->asg/dot_general | solution.py:25
  23.0 1.9 %collective-permute-start = (f32[48,16,32]{0,1,2:T(8,128)S(1)}, f32[48,16,32]{0,1,2:T(8,128)S(1)}, u32[]{:S(2)}, u32[]{:S(2)}) collective-permute-start(f32[48,16,32]{0,1,2:T(8,128)S(1)} %fusion.10), channel_id=1, source_target_pairs={{0,1},{1,0},{2,3},{3,2},{4,5},{5,4},{6,7},{7,6},{8,9},{9,8},{10,11... | collective-permute-start | bytes 294920 | tf_op jit(solution)/shard_map/ppermute | solution.py:14
  24.9 2.9 %fusion.16 = f32[32,16,48]{2,1,0:T(8,128)S(1)} fusion(f32[48,16,32]{0,1,2:T(8,128)S(1)} %fusion.10, f32[1,1,48,48,32]{3,4,2,1,0:T(8,128)} %get-tuple-element.16), kind=kOutput, calls=%fused_computation.37 | convolution fusion | flops 14155776 | bytes 491520 | tf_op jit(solution)/shard_map/abg,bsg->asg/dot_general | solution.py:24
  27.8 3.4 %collective-permute-done = f32[48,16,32]{0,1,2:T(8,128)S(1)} collective-permute-done((f32[48,16,32]{0,1,2:T(8,128)S(1)}, f32[48,16,32]{0,1,2:T(8,128)S(1)}, u32[]{:S(2)}, u32[]{:S(2)}) %collective-permute-start) | collective-permute-done | bytes 98336 | tf_op jit(solution)/shard_map/ppermute | solution.py:14
  31.2 0.0 copy-start.4
  31.2 2.9 %fusion.9 = f32[48,16,32]{0,1,2:T(8,128)S(1)} fusion(f32[32,16,48]{2,1,0:T(8,128)S(1)} %fusion.16, f32[48,16,32]{0,1,2:T(8,128)S(1)} %collective-permute-done, f32[1,1,48,48,32]{3,4,2,1,0:T(8,128)} %get-tuple-element.15), kind=kOutput, calls=%fused_computation.17 | convolution fusion | flops 14180352 | bytes 589824 | tf_op jit(solution)/shard_map/abg,bsg->asg/dot_general | solution.py:25
  34.1 3.4 %collective-permute-start.1 = (f32[48,16,32]{0,1,2:T(8,128)S(1)}, f32[48,16,32]{0,1,2:T(8,128)S(1)}, u32[]{:S(2)}, u32[]{:S(2)}) collective-permute-start(f32[48,16,32]{0,1,2:T(8,128)S(1)} %fusion.9), channel_id=1, source_target_pairs={{0,2},{2,0},{1,3},{3,1},{4,6},{6,4},{5,7},{7,5},{8,10},{10,8},{9,1... | collective-permute-start | bytes 294920 | tf_op jit(solution)/shard_map/ppermute | solution.py:14
  37.5 0.0 copy-start.3
  37.5 2.9 %fusion.15 = f32[32,16,48]{2,1,0:T(8,128)S(1)} fusion(f32[48,16,32]{0,1,2:T(8,128)S(1)} %fusion.9, f32[1,1,48,48,32]{3,4,2,1,0:T(8,128)} %get-tuple-element.14), kind=kOutput, calls=%fused_computation.34 | convolution fusion | flops 14155776 | bytes 491520 | tf_op jit(solution)/shard_map/abg,bsg->asg/dot_general | solution.py:24
  40.4 2.5 %collective-permute-done.1 = f32[48,16,32]{0,1,2:T(8,128)S(1)} collective-permute-done((f32[48,16,32]{0,1,2:T(8,128)S(1)}, f32[48,16,32]{0,1,2:T(8,128)S(1)}, u32[]{:S(2)}, u32[]{:S(2)}) %collective-permute-start.1) | collective-permute-done | bytes 98336 | tf_op jit(solution)/shard_map/ppermute | solution.py:14
  43.0 0.0 copy-done.11
  43.0 0.0 copy-start.2
  43.0 1.7 %fusion.8 = f32[48,16,32]{0,1,2:T(8,128)S(1)} fusion(f32[32,16,48]{2,1,0:T(8,128)S(1)} %fusion.15, f32[48,16,32]{0,1,2:T(8,128)S(1)} %collective-permute-done.1, f32[1,1,48,48,32]{3,4,2,1,0:T(8,128)S(1)} %copy-done.11), kind=kOutput, calls=%fused_computation.15 | convolution fusion | flops 14180352 | bytes 589824 | tf_op jit(solution)/shard_map/abg,bsg->asg/dot_general | solution.py:25
  44.7 2.0 %collective-permute-start.2 = (f32[48,16,32]{0,1,2:T(8,128)S(1)}, f32[48,16,32]{0,1,2:T(8,128)S(1)}, u32[]{:S(2)}, u32[]{:S(2)}) collective-permute-start(f32[48,16,32]{0,1,2:T(8,128)S(1)} %fusion.8), channel_id=1, source_target_pairs={{0,4},{4,0},{1,5},{5,1},{2,6},{6,2},{3,7},{7,3},{8,12},{12,8},{9,1... | collective-permute-start | bytes 294920 | tf_op jit(solution)/shard_map/ppermute | solution.py:14
  46.7 0.0 copy-done.10
  46.7 1.7 %fusion.14 = f32[32,16,48]{2,1,0:T(8,128)S(1)} fusion(f32[48,16,32]{0,1,2:T(8,128)S(1)} %fusion.8, f32[1,1,48,48,32]{3,4,2,1,0:T(8,128)S(1)} %copy-done.10), kind=kOutput, calls=%fused_computation.31 | convolution fusion | flops 14155776 | bytes 491520 | tf_op jit(solution)/shard_map/abg,bsg->asg/dot_general | solution.py:24
  48.4 2.8 %collective-permute-done.2 = f32[48,16,32]{0,1,2:T(8,128)S(1)} collective-permute-done((f32[48,16,32]{0,1,2:T(8,128)S(1)}, f32[48,16,32]{0,1,2:T(8,128)S(1)}, u32[]{:S(2)}, u32[]{:S(2)}) %collective-permute-start.2) | collective-permute-done | bytes 98336 | tf_op jit(solution)/shard_map/ppermute | solution.py:14
  51.2 0.0 copy-done.9
  51.2 1.7 %fusion.7 = f32[48,16,32]{0,1,2:T(8,128)S(1)} fusion(f32[32,16,48]{2,1,0:T(8,128)S(1)} %fusion.14, f32[48,16,32]{0,1,2:T(8,128)S(1)} %collective-permute-done.2, f32[1,1,48,48,32]{3,4,2,1,0:T(8,128)S(1)} %copy-done.9), kind=kOutput, calls=%fused_computation.13 | convolution fusion | flops 14180352 | bytes 589824 | tf_op jit(solution)/shard_map/abg,bsg->asg/dot_general | solution.py:25
  52.9 4.1 %collective-permute-start.3 = (f32[48,16,32]{0,1,2:T(8,128)S(1)}, f32[48,16,32]{0,1,2:T(8,128)S(1)}, u32[]{:S(2)}, u32[]{:S(2)}) collective-permute-start(f32[48,16,32]{0,1,2:T(8,128)S(1)} %fusion.7), channel_id=1, source_target_pairs={{0,8},{8,0},{1,9},{9,1},{2,10},{10,2},{3,11},{11,3},{4,12},{12,4},... | collective-permute-start | bytes 294920 | tf_op jit(solution)/shard_map/ppermute | solution.py:14
  57.0 0.0 copy-done.8
  57.0 1.7 %fusion.13 = f32[32,16,48]{2,1,0:T(8,128)S(1)} fusion(f32[48,16,32]{0,1,2:T(8,128)S(1)} %fusion.7, f32[1,1,48,48,32]{3,4,2,1,0:T(8,128)S(1)} %copy-done.8), kind=kOutput, calls=%fused_computation.28 | convolution fusion | flops 14155776 | bytes 491520 | tf_op jit(solution)/shard_map/abg,bsg->asg/dot_general | solution.py:24
  58.7 2.7 %collective-permute-done.3 = f32[48,16,32]{0,1,2:T(8,128)S(1)} collective-permute-done((f32[48,16,32]{0,1,2:T(8,128)S(1)}, f32[48,16,32]{0,1,2:T(8,128)S(1)}, u32[]{:S(2)}, u32[]{:S(2)}) %collective-permute-start.3) | collective-permute-done | bytes 98336 | tf_op jit(solution)/shard_map/ppermute | solution.py:14
  61.4 0.0 copy-done.7
  61.4 1.7 %fusion.6 = f32[48,16,32]{0,1,2:T(8,128)S(1)} fusion(f32[32,16,48]{2,1,0:T(8,128)S(1)} %fusion.13, f32[48,16,32]{0,1,2:T(8,128)S(1)} %collective-permute-done.3, f32[1,1,48,48,32]{3,4,2,1,0:T(8,128)S(1)} %copy-done.7), kind=kOutput, calls=%fused_computation.11 | convolution fusion | flops 14180352 | bytes 589824 | tf_op jit(solution)/shard_map/abg,bsg->asg/dot_general | solution.py:25
  63.1 0.1 collective-permute-start.4
  63.2 0.0 copy-done.6
  63.2 1.7 %fusion.12 = f32[32,16,48]{2,1,0:T(8,128)S(1)} fusion(f32[48,16,32]{0,1,2:T(8,128)S(1)} %fusion.6, f32[1,1,48,48,32]{3,4,2,1,0:T(8,128)S(1)} %copy-done.6), kind=kOutput, calls=%fused_computation.25 | convolution fusion | flops 14155776 | bytes 491520 | tf_op jit(solution)/shard_map/abg,bsg->asg/dot_general | solution.py:24
  64.9 0.0 collective-permute-done.4
  64.9 0.0 copy-done.5
  64.9 1.7 %fusion.5 = f32[48,16,32]{0,1,2:T(8,128)S(1)} fusion(f32[32,16,48]{2,1,0:T(8,128)S(1)} %fusion.12, f32[48,16,32]{0,1,2:T(8,128)S(1)} %collective-permute-done.4, f32[1,1,48,48,32]{3,4,2,1,0:T(8,128)S(1)} %copy-done.5), kind=kOutput, calls=%fused_computation.9 | convolution fusion | flops 14180352 | bytes 589824 | tf_op jit(solution)/shard_map/abg,bsg->asg/dot_general | solution.py:25
  66.6 1.6 %collective-permute-start.5 = (f32[48,16,32]{0,1,2:T(8,128)S(1)}, f32[48,16,32]{0,1,2:T(8,128)S(1)}, u32[]{:S(2)}, u32[]{:S(2)}) collective-permute-start(f32[48,16,32]{0,1,2:T(8,128)S(1)} %fusion.5), channel_id=1, source_target_pairs={{0,32},{32,0},{16,48},{48,16},{64,96},{96,64},{80,112},{112,80},{1... | collective-permute-start | bytes 294920 | tf_op jit(solution)/shard_map/ppermute | solution.py:14
  68.2 0.0 copy-done.4
  68.2 1.7 %fusion.11 = f32[32,16,48]{2,1,0:T(8,128)S(1)} fusion(f32[48,16,32]{0,1,2:T(8,128)S(1)} %fusion.5, f32[1,1,48,48,32]{3,4,2,1,0:T(8,128)S(1)} %copy-done.4), kind=kOutput, calls=%fused_computation.22 | convolution fusion | flops 14155776 | bytes 491520 | tf_op jit(solution)/shard_map/abg,bsg->asg/dot_general | solution.py:24
  69.8 5.5 %collective-permute-done.5 = f32[48,16,32]{0,1,2:T(8,128)S(1)} collective-permute-done((f32[48,16,32]{0,1,2:T(8,128)S(1)}, f32[48,16,32]{0,1,2:T(8,128)S(1)}, u32[]{:S(2)}, u32[]{:S(2)}) %collective-permute-start.5) | collective-permute-done | bytes 98336 | tf_op jit(solution)/shard_map/ppermute | solution.py:14
  75.4 0.0 copy-done.3
  75.4 1.7 %fusion.4 = f32[48,16,32]{0,1,2:T(8,128)S(1)} fusion(f32[32,16,48]{2,1,0:T(8,128)S(1)} %fusion.11, f32[48,16,32]{0,1,2:T(8,128)S(1)} %collective-permute-done.5, f32[1,1,48,48,32]{3,4,2,1,0:T(8,128)S(1)} %copy-done.3), kind=kOutput, calls=%fused_computation.7 | convolution fusion | flops 14180352 | bytes 589824 | tf_op jit(solution)/shard_map/abg,bsg->asg/dot_general | solution.py:25
  77.1 3.4 %collective-permute-start.6 = (f32[48,16,32]{0,1,2:T(8,128)S(1)}, f32[48,16,32]{0,1,2:T(8,128)S(1)}, u32[]{:S(2)}, u32[]{:S(2)}) collective-permute-start(f32[48,16,32]{0,1,2:T(8,128)S(1)} %fusion.4), channel_id=1, source_target_pairs={{0,64},{64,0},{16,80},{80,16},{32,96},{96,32},{48,112},{112,48},{1... | collective-permute-start | bytes 294920 | tf_op jit(solution)/shard_map/ppermute | solution.py:14
  80.4 0.0 copy-done.2
  80.4 1.7 %fusion.19 = f32[32,16,48]{2,1,0:T(8,128)S(1)} fusion(f32[48,16,32]{0,1,2:T(8,128)S(1)} %fusion.4, f32[48,48,32]{1,2,0:T(8,128)S(1)} %copy-done.2), kind=kOutput, calls=%fused_computation.42 | convolution fusion | flops 14155776 | bytes 491520 | tf_op jit(solution)/shard_map/abg,bsg->asg/dot_general | solution.py:24
  82.1 4.7 %collective-permute-done.6 = f32[48,16,32]{0,1,2:T(8,128)S(1)} collective-permute-done((f32[48,16,32]{0,1,2:T(8,128)S(1)}, f32[48,16,32]{0,1,2:T(8,128)S(1)}, u32[]{:S(2)}, u32[]{:S(2)}) %collective-permute-start.6) | collective-permute-done | bytes 98336 | tf_op jit(solution)/shard_map/ppermute | solution.py:14
  86.8 0.0 copy-done.1
  86.8 1.7 %fusion.22 = f32[32,16,48]{2,1,0:T(8,128)S(1)} fusion(f32[32,16,48]{2,1,0:T(8,128)S(1)} %fusion.19, f32[48,16,32]{0,1,2:T(8,128)S(1)} %collective-permute-done.6, f32[48,48,32]{1,2,0:T(8,128)S(1)} %copy-done.1), kind=kOutput, calls=%fused_computation.47 | convolution fusion | flops 14180352 | bytes 589824 | tf_op jit(solution)/shard_map/abg,bsg->asg/dot_general | solution.py:25
  88.5 0.2 reshape.48
  88.8 15.3 %all_to_all.5 = f32[16,1,1536]{2,1,0:T(1,128)S(1)} all-to-all(f32[16,1,1536]{2,1,0:T(1,128)S(1)} %reshape.48), channel_id=1, replica_groups=mesh['gx'=8,'gy'=16] {'gy'}, dimensions={0} | all-to-all | bytes 196608 | tf_op jit(solution)/shard_map/all_to_all | solution.py:49
  104.1 0.5 broadcast
  104.6 0.9 reduce
  105.5 0.1 reshape.49
  105.6 5.2 %convolution_bitcast_fusion = f32[32,2,8,1024]{3,2,1,0:T(8,128)S(1)} fusion(f32[32,48,1024]{2,1,0:T(8,128)} %param.7, f32[32,16,48]{2,1,0:T(8,128)S(1)} %reshape.49), kind=kOutput, calls=%fused_computation.3 | convolution fusion | flops 301989888 | bytes 8486912 | tf_op jit(solution)/shard_map/grp,rsg->sgp/dot_general | solution.py:50
  110.8 1.5 %copy.53 = f32[32,2,8,1024]{3,2,0,1:T(8,128)} copy(f32[32,2,8,1024]{3,2,1,0:T(8,128)S(1)} %convolution_bitcast_fusion) | data formatting | bytes 4194304 | tf_op jit(solution)/shard_map/reshape | solution.py:51
  (2 shorter events, 0.0 us)
Async XLA Ops:
  0.0 9.6 %copy-start = (f32[32,48,1024]{2,1,0:T(8,128)S(1)}, f32[32,48,1024]{2,1,0:T(8,128)}, u32[]{:S(2)}) copy-start(f32[32,48,1024]{2,1,0:T(8,128)} %param.5) | copy-start | bytes 18874372
  9.6 7.2 %copy-start.12 = (f32[1,1,48,48,32]{3,4,2,1,0:T(8,128)S(1)}, f32[1,1,48,48,32]{3,4,2,1,0:T(8,128)}, u32[]{:S(2)}) copy-start(f32[1,1,48,48,32]{3,4,2,1,0:T(8,128)} %get-tuple-element.18) | copy-start | bytes 884740
  16.8 29.9 %copy-start.10 = (f32[1,1,48,48,32]{3,4,2,1,0:T(8,128)S(1)}, f32[1,1,48,48,32]{3,4,2,1,0:T(8,128)}, u32[]{:S(2)}) copy-start(f32[1,1,48,48,32]{3,4,2,1,0:T(8,128)} %get-tuple-element.12) | copy-start | bytes 884740
  16.8 34.5 %copy-start.9 = (f32[1,1,48,48,32]{3,4,2,1,0:T(8,128)S(1)}, f32[1,1,48,48,32]{3,4,2,1,0:T(8,128)}, u32[]{:S(2)}) copy-start(f32[1,1,48,48,32]{3,4,2,1,0:T(8,128)} %get-tuple-element.11) | copy-start | bytes 884740
  16.8 40.3 %copy-start.8 = (f32[1,1,48,48,32]{3,4,2,1,0:T(8,128)S(1)}, f32[1,1,48,48,32]{3,4,2,1,0:T(8,128)}, u32[]{:S(2)}) copy-start(f32[1,1,48,48,32]{3,4,2,1,0:T(8,128)} %get-tuple-element.10) | copy-start | bytes 884740
  19.2 42.2 %copy-start.7 = (f32[1,1,48,48,32]{3,4,2,1,0:T(8,128)S(1)}, f32[1,1,48,48,32]{3,4,2,1,0:T(8,128)}, u32[]{:S(2)}) copy-start(f32[1,1,48,48,32]{3,4,2,1,0:T(8,128)} %get-tuple-element.9) | copy-start | bytes 884740
  19.9 23.1 %copy-start.11 = (f32[1,1,48,48,32]{3,4,2,1,0:T(8,128)S(1)}, f32[1,1,48,48,32]{3,4,2,1,0:T(8,128)}, u32[]{:S(2)}) copy-start(f32[1,1,48,48,32]{3,4,2,1,0:T(8,128)} %get-tuple-element.13) | copy-start | bytes 884740
  19.9 43.3 %copy-start.6 = (f32[1,1,48,48,32]{3,4,2,1,0:T(8,128)S(1)}, f32[1,1,48,48,32]{3,4,2,1,0:T(8,128)}, u32[]{:S(2)}) copy-start(f32[1,1,48,48,32]{3,4,2,1,0:T(8,128)} %get-tuple-element.8) | copy-start | bytes 884740
  23.0 8.2 %collective-permute-start = (f32[48,16,32]{0,1,2:T(8,128)S(1)}, f32[48,16,32]{0,1,2:T(8,128)S(1)}, u32[]{:S(2)}, u32[]{:S(2)}) collective-permute-start(f32[48,16,32]{0,1,2:T(8,128)S(1)} %fusion.10), channel_id=1, source_target_pairs={{0,1},{1,0},{2,3},{3,2},{4,5},{5,4},{6,7},{7,6},{8,9},{9,8},{10,11... | collective-permute-start | bytes 294920 | tf_op jit(solution)/shard_map/ppermute | solution.py:14
  24.9 40.0 %copy-start.5 = (f32[1,1,48,48,32]{3,4,2,1,0:T(8,128)S(1)}, f32[1,1,48,48,32]{3,4,2,1,0:T(8,128)}, u32[]{:S(2)}) copy-start(f32[1,1,48,48,32]{3,4,2,1,0:T(8,128)} %get-tuple-element.7) | copy-start | bytes 884740
  31.2 37.0 %copy-start.4 = (f32[1,1,48,48,32]{3,4,2,1,0:T(8,128)S(1)}, f32[1,1,48,48,32]{3,4,2,1,0:T(8,128)}, u32[]{:S(2)}) copy-start(f32[1,1,48,48,32]{3,4,2,1,0:T(8,128)} %get-tuple-element.6) | copy-start | bytes 884740
  34.1 8.9 %collective-permute-start.1 = (f32[48,16,32]{0,1,2:T(8,128)S(1)}, f32[48,16,32]{0,1,2:T(8,128)S(1)}, u32[]{:S(2)}, u32[]{:S(2)}) collective-permute-start(f32[48,16,32]{0,1,2:T(8,128)S(1)} %fusion.9), channel_id=1, source_target_pairs={{0,2},{2,0},{1,3},{3,1},{4,6},{6,4},{5,7},{7,5},{8,10},{10,8},{9,1... | collective-permute-start | bytes 294920 | tf_op jit(solution)/shard_map/ppermute | solution.py:14
  37.5 37.8 %copy-start.3 = (f32[1,1,48,48,32]{3,4,2,1,0:T(8,128)S(1)}, f32[1,1,48,48,32]{3,4,2,1,0:T(8,128)}, u32[]{:S(2)}) copy-start(f32[1,1,48,48,32]{3,4,2,1,0:T(8,128)} %get-tuple-element.19) | copy-start | bytes 884740
  43.0 37.5 %copy-start.2 = (f32[48,48,32]{1,2,0:T(8,128)S(1)}, f32[48,48,32]{1,2,0:T(8,128)}, u32[]{:S(2)}) copy-start(f32[48,48,32]{1,2,0:T(8,128)} %get-tuple-element.20) | copy-start | bytes 884740
  44.7 6.6 %collective-permute-start.2 = (f32[48,16,32]{0,1,2:T(8,128)S(1)}, f32[48,16,32]{0,1,2:T(8,128)S(1)}, u32[]{:S(2)}, u32[]{:S(2)}) collective-permute-start(f32[48,16,32]{0,1,2:T(8,128)S(1)} %fusion.8), channel_id=1, source_target_pairs={{0,4},{4,0},{1,5},{5,1},{2,6},{6,2},{3,7},{7,3},{8,12},{12,8},{9,1... | collective-permute-start | bytes 294920 | tf_op jit(solution)/shard_map/ppermute | solution.py:14
  46.7 40.1 %copy-start.1 = (f32[48,48,32]{1,2,0:T(8,128)S(1)}, f32[48,48,32]{1,2,0:T(8,128)}, u32[]{:S(2)}) copy-start(f32[48,48,32]{1,2,0:T(8,128)} %get-tuple-element.5) | copy-start | bytes 884740
  52.9 8.5 %collective-permute-start.3 = (f32[48,16,32]{0,1,2:T(8,128)S(1)}, f32[48,16,32]{0,1,2:T(8,128)S(1)}, u32[]{:S(2)}, u32[]{:S(2)}) collective-permute-start(f32[48,16,32]{0,1,2:T(8,128)S(1)} %fusion.7), channel_id=1, source_target_pairs={{0,8},{8,0},{1,9},{9,1},{2,10},{10,2},{3,11},{11,3},{4,12},{12,4},... | collective-permute-start | bytes 294920 | tf_op jit(solution)/shard_map/ppermute | solution.py:14
  63.1 1.8 %collective-permute-start.4 = (f32[48,16,32]{0,1,2:T(8,128)S(1)}, f32[48,16,32]{0,1,2:T(8,128)S(1)}, u32[]{:S(2)}, u32[]{:S(2)}) collective-permute-start(f32[48,16,32]{0,1,2:T(8,128)S(1)} %fusion.6), channel_id=1, source_target_pairs={{0,16},{16,0},{32,48},{48,32},{64,80},{80,64},{96,112},{112,96},{1... | collective-permute-start | bytes 294920 | tf_op jit(solution)/shard_map/ppermute | solution.py:14
  66.6 8.8 %collective-permute-start.5 = (f32[48,16,32]{0,1,2:T(8,128)S(1)}, f32[48,16,32]{0,1,2:T(8,128)S(1)}, u32[]{:S(2)}, u32[]{:S(2)}) collective-permute-start(f32[48,16,32]{0,1,2:T(8,128)S(1)} %fusion.5), channel_id=1, source_target_pairs={{0,32},{32,0},{16,48},{48,16},{64,96},{96,64},{80,112},{112,80},{1... | collective-permute-start | bytes 294920 | tf_op jit(solution)/shard_map/ppermute | solution.py:14
  77.1 9.8 %collective-permute-start.6 = (f32[48,16,32]{0,1,2:T(8,128)S(1)}, f32[48,16,32]{0,1,2:T(8,128)S(1)}, u32[]{:S(2)}, u32[]{:S(2)}) collective-permute-start(f32[48,16,32]{0,1,2:T(8,128)S(1)} %fusion.4), channel_id=1, source_target_pairs={{0,64},{64,0},{16,80},{80,16},{32,96},{96,32},{48,112},{112,48},{1... | collective-permute-start | bytes 294920 | tf_op jit(solution)/shard_map/ppermute | solution.py:14
where the time goes:
time: 113 us; the launch traced here: 112 us
  matrix products  45 us (40%)
  waiting for transfers between devices  21.7 us (19%)
  starting transfers between devices  16.5 us (15%)
  blocking collectives  15.3 us (14%)
  local copies, waits for them, and re-layouts  12.7 us (11%)
    ppermute x7, waiting for transfers between devices, swapped(): return lax.ppermute(block, axis, route)  21.7 us
    dot_general x8, matrix products, combine(): jnp.einsum('abg,bsg->asg', blocks[0], state, precision=lax.Precision.HIGH...  16.6 us
    ppermute x7, starting transfers between devices, swapped(): return lax.ppermute(block, axis, route)  16.5 us
    dot_general x8, matrix products, combine(): jnp.einsum('abg,bsg->asg', blocks[1], other, precision=lax.Precision.HIGH...  16.1 us
    all_to_all x1, blocking collectives, body(): moved = lax.all_to_all(state, 'gy', split_axis=2, concat_axis=2, tiled=True)  15.3 us
    squeeze x1, local copies, waits for them, and re-layouts, combine(): blocks[1]  9.56 us
    dot_general x1, matrix products, body(): jnp.einsum('sgp,grp->rsg', points, leaf_basis, precision=lax.Precision.HI...  7.19 us
    dot_general x1, matrix products, body(): jnp.einsum('grp,rsg->sgp', out_basis, moved, precision=lax.Precision.HIGH...  5.19 us
  transfers between devices with their start and end apart: 7, of which 6 were waited for; matrix products, arithmetic and copies ran while one was open for 13% of the time, Pallas kernels for 0%

commit v1 on v0

v1 whole, which is shorter than its diff:
```python
import functools

import jax
import jax.numpy as jnp
from jax import lax
from jax.experimental import pallas as pl
from jax.experimental.pallas import tpu as pltpu
from jax.sharding import PartitionSpec as P

F32 = jnp.float32
BF16 = jnp.bfloat16
LANES = 128
CHUNK = 4


def flipped(index, bit):
    return index + bit * (1 - 2 * (lax.div(index, bit) % 2))


def crossed(index, mask):
    bit = 1
    while bit <= mask:
        if mask & bit:
            index = flipped(index, bit)
        bit *= 2
    return index


def split(value):
    high = value.astype(BF16)
    return high, (value - high.astype(F32)).astype(BF16)


def stacked(value):
    high, low = split(value)
    return jnp.concatenate(
        [
            jnp.concatenate([high, high], 1),
            jnp.concatenate([low, jnp.zeros_like(low)], 1),
        ],
        0,
    )


def across(left, right):
    return lax.dot_general(left, right, (((1,), (1,)), ((), ())), preferred_element_type=F32)


def kernel(
    n_gx, n_gy, rank,
    src, leaf, blocks, basis, out,
    src_v, leaf_v, raw, tiles, state, far, moved, wide,
    src_sem, leaf_sem, raw_sem, basis_sem, send_sem, recv_sem, out_sem, in_sem,
):
    pairs = leaf.shape[0]
    count = src.shape[0]
    points = leaf.shape[2]
    levels = blocks.shape[0] // 2
    chunks = pairs // CHUNK
    both = 2 * rank
    gx, gy = lax.axis_index("gx"), lax.axis_index("gy")
    lane = lax.broadcasted_iota(jnp.int32, (count, both), 1)
    first_box = lane < rank

    def partner(level):
        bit = 2 ** (level - 1)
        if bit < n_gy:
            return gx, flipped(gy, bit)
        return flipped(gx, bit // n_gy), gy

    def src_copy(j):
        width = CHUNK * 2 * points
        return pltpu.make_async_copy(
            src.at[:, pl.ds(pl.multiple_of(j * width, width), width)], src_v.at[j], src_sem.at[j]
        )

    def leaf_copy(j):
        part = pl.ds(j * CHUNK, CHUNK)
        return pltpu.make_async_copy(leaf.at[part], leaf_v.at[part], leaf_sem.at[j])

    def basis_copy(j):
        part = pl.ds(j * CHUNK, CHUNK)
        return pltpu.make_async_copy(basis.at[part], leaf_v.at[part], basis_sem.at[j])

    def raw_copy(i):
        return pltpu.make_async_copy(blocks.at[i], raw.at[i], raw_sem.at[i])

    def exchange(level, j):
        part = pl.ds(j * CHUNK, CHUNK)
        return pltpu.make_async_remote_copy(
            src_ref=state.at[level, part],
            dst_ref=far.at[level, part],
            send_sem=send_sem.at[level, j],
            recv_sem=recv_sem.at[level, j],
            device_id=partner(level),
            device_id_type=pl.DeviceIdType.MESH,
        )

    def handover(b):
        return pltpu.make_async_remote_copy(
            src_ref=state.at[levels, b],
            dst_ref=moved.at[gy],
            send_sem=out_sem.at[b],
            recv_sem=in_sem.at[gy],
            device_id=(gx, b),
            device_id_type=pl.DeviceIdType.MESH,
        )

    def arrival(a):
        return pltpu.make_async_remote_copy(
            src_ref=state.at[levels, a],
            dst_ref=moved.at[a],
            send_sem=out_sem.at[a],
            recv_sem=in_sem.at[a],
            device_id=(gx, a),
            device_id_type=pl.DeviceIdType.MESH,
        )

    barrier = pltpu.get_barrier_semaphore()
    for level in range(1, levels):
        pl.semaphore_signal(barrier, inc=1, device_id=partner(level), device_id_type=pl.DeviceIdType.MESH)

    raw_copy(0).start()
    raw_copy(1).start()
    ahead = 2
    for j in range(min(ahead, chunks)):
        src_copy(j).start()
        leaf_copy(j).start()

    def blank(i, carry):
        state[i] = jnp.zeros_like(state[i])
        return carry

    lax.fori_loop(0, levels + 1, blank, 0)

    def lay(level, which, p):
        gap = jnp.zeros((rank, LANES - both), F32)
        empty = jnp.zeros((rank, rank), F32)
        total = 2 * pairs
        for c in range(2):
            own = raw[2 * level + which, pl.ds(2 * p + c, rank, stride=total), :]
            if level == 0:
                other = raw[1, pl.ds(2 * p + c, rank, stride=total), :]
            else:
                other = empty
            full = jnp.concatenate([own, other, gap] if c == 0 else [other, own, gap], 1)
            high, low = split(full)
            tiles[level, which, p, c * rank : (c + 1) * rank, :LANES] = high
            tiles[level, which, p, c * rank : (c + 1) * rank, LANES:] = low

    def lay_level(level):
        def step(i, carry):
            for q in range(2):
                for which in range(1 if level == 0 else 2):
                    lay(level, which, 2 * i + q)
            return carry

        raw_copy(2 * level).wait()
        raw_copy(2 * level + 1).wait()
        lax.fori_loop(0, pairs // 2, step, 0)

    lay_level(0)

    def compress(j, carry):
        src_copy(j).wait()
        leaf_copy(j).wait()

        @pl.when(j + ahead < chunks)
        def _():
            src_copy(j + ahead).start()
            leaf_copy(j + ahead).start()

        for q in range(CHUNK):
            p = j * CHUNK + q
            high, low = split(leaf_v[p])
            h0, l0 = split(src_v[j, :, 2 * q * points : (2 * q + 1) * points])
            h1, l1 = split(src_v[j, :, (2 * q + 1) * points : (2 * q + 2) * points])
            main = across(jnp.concatenate([h0, h1, l0, l1], 0), high)
            rest = across(jnp.concatenate([h0, h1], 0), low)
            total = main[: 2 * count] + main[2 * count :] + rest
            state[0, p, :, :both] = jnp.where(first_box, total[:count], total[count:])
        for q in range(CHUNK):
            p = j * CHUNK + q
            product = across(stacked(state[0, p]), tiles[0, 0, p])
            state[1, p, :, :both] = product[:count] + product[count:]

        @pl.when(j == 0)
        def _():
            pl.semaphore_wait(barrier, levels - 1)

        exchange(1, j).start()
        return carry

    lax.fori_loop(0, chunks, compress, 0)
    for i in range(2, 2 * levels):
        raw_copy(i).start()
    for j in range(chunks):
        basis_copy(j).start()
    lay_level(1)

    for level in range(1, levels):

        def combine(j, carry, level=level):
            exchange(level, j).wait_recv()
            for q in range(CHUNK):
                p = j * CHUNK + q
                product = across(stacked(state[level, p]), tiles[level, 0, p])
                product += across(stacked(far[level, p]), tiles[level, 1, p])
                state[level + 1, p, :, :both] = product[:count] + product[count:]
            if level + 1 < levels:
                exchange(level + 1, j).start()
            else:
                for q in range(CHUNK):
                    b = j * CHUNK + q

                    @pl.when(b != gy)
                    def _():
                        handover(b).start()

            return carry

        lax.fori_loop(0, chunks, combine, 0)
        if level + 1 < levels:
            lay_level(level + 1)
        if level == 1:

            def spread(j, carry):
                basis_copy(j).wait()
                for q in range(CHUNK):
                    p = j * CHUNK + q
                    high, low = split(leaf_v[p])
                    wide[p, :both] = high
                    wide[p, both:] = low
                return carry

            lax.fori_loop(0, chunks, spread, 0)

    moved[gy] = state[levels, gy]
    hops = [0, 1, 2, 1]
    order = sorted(range(n_gy), key=lambda d: hops[d % 4] + hops[d // 4 % 4])
    for d in order:
        a = crossed(gy, d)
        if d:
            arrival(a).wait_recv()
        high, low = split(moved[a][:, :both])
        none = jnp.zeros_like(high)
        rows = []
        for mine in (first_box, jnp.logical_not(first_box)):
            kept = jnp.where(mine, high, none)
            rows.append(jnp.concatenate([kept, kept], 1))
            rows.append(jnp.concatenate([jnp.where(mine, low, none), none], 1))
        product = jnp.dot(jnp.concatenate(rows, 0), wide[a], preferred_element_type=F32)
        for c in range(2):
            at = pl.multiple_of((2 * a + c) * points, points)
            out[:, pl.ds(at, points)] = (
                product[2 * c * count : (2 * c + 1) * count]
                + product[(2 * c + 1) * count : (2 * c + 2) * count]
            )

    def drain(j, carry):
        for level in range(1, levels):
            exchange(level, j).wait_send()
        return carry

    lax.fori_loop(0, chunks, drain, 0)

    def drain_out(b, carry):
        @pl.when(b != gy)
        def _():
            handover(b).wait_send()

        return carry

    lax.fori_loop(0, n_gy, drain_out, 0)


def body(n_gx, n_gy, sources, leaf_basis, level_blocks, out_basis):
    boxes, rank, points = leaf_basis.shape
    count = sources.shape[0]
    levels = level_blocks.shape[0]
    pairs = boxes // 2
    chunks = pairs // CHUNK
    leaf = leaf_basis.reshape(pairs, 2 * rank, points)
    basis = out_basis.reshape(pairs, 2 * rank, points)
    blocks = level_blocks.transpose(0, 1, 2, 4, 3).reshape(2 * levels, rank * boxes, rank)
    dma = pltpu.SemaphoreType.DMA
    anywhere = pl.BlockSpec(memory_space=pl.ANY)
    return pl.pallas_call(
        functools.partial(kernel, n_gx, n_gy, rank),
        out_shape=jax.ShapeDtypeStruct((count, boxes * points), F32),
        in_specs=[anywhere] * 4,
        out_specs=pl.BlockSpec(memory_space=pltpu.VMEM),
        scratch_shapes=[
            pltpu.VMEM((chunks, count, CHUNK * 2 * points), F32),
            pltpu.VMEM((pairs, 2 * rank, points), F32),
            pltpu.VMEM((2 * levels, rank * boxes, rank), F32),
            pltpu.VMEM((levels, 2, pairs, 2 * rank, 2 * LANES), BF16),
            pltpu.VMEM((levels + 1, pairs, count, LANES), F32),
            pltpu.VMEM((levels, pairs, count, LANES), F32),
            pltpu.VMEM((n_gy, count, LANES), F32),
            pltpu.VMEM((pairs, 4 * rank, points), BF16),
            dma((chunks,)),
            dma((chunks,)),
            dma((2 * levels,)),
            dma((chunks,)),
            dma((levels, chunks)),
            dma((levels, chunks)),
            dma((n_gy,)),
            dma((n_gy,)),
        ],
        compiler_params=pltpu.CompilerParams(
            collective_id=0, has_side_effects=True, vmem_limit_bytes=60 * 2**20
        ),
        name="sweep",
    )(sources, leaf, blocks, basis)


def solution(mesh):
    placed = (
        P(None, ("gx", "gy")),
        P(("gx", "gy"), None, None),
        P(None, None, None, None, ("gx", "gy")),
        P(("gx", "gy"), None, None),
    )
    return jax.shard_map(
        functools.partial(body, mesh.shape["gx"], mesh.shape["gy"]),
        mesh=mesh, in_specs=placed, out_specs=P(None, ("gx", "gy")), check_vma=False,
    )
```

time: 113 us -> 48.4 us (0.43)
  Pallas kernels: 0 us -> 45.1 us
  matrix products: 45 us -> 0 us
  waiting for transfers between devices: 21.7 us -> 0 us
  starting transfers between devices: 16.5 us -> 0 us
  blocking collectives: 15.3 us -> 0 us
  local copies, waits for them, and re-layouts: 12.7 us -> 3.05 us
    pallas_call x0 -> x1, Pallas kernels: none -> 45.1 us  [body(): pl.pallas_call(functools.partial(kernel, n_gx, n_gy, rank), out_shape=jax...]
    dot_general x18 -> x0, matrix products: 45 us -> none  [the longest x8 16.6 us: combine(): jnp.einsum('abg,bsg->asg', blocks[0], state, precision=lax.Precision.HIGH...]
    ppermute x7 -> x0, waiting for transfers between devices: 21.7 us -> none  [swapped(): return lax.ppermute(block, axis, route)]
    ppermute x7 -> x0, starting transfers between devices: 16.5 us -> none  [swapped(): return lax.ppermute(block, axis, route)]
    all_to_all x1 -> x0, blocking collectives: 15.3 us -> none  [body(): moved = lax.all_to_all(state, 'gy', split_axis=2, concat_axis=2, tiled=True)]
    squeeze x1 -> x0, local copies, waits for them, and re-layouts: 9.56 us -> none  [combine(): blocks[1]]
    unnamed x28 -> x1, local copies, waits for them, and re-layouts: 0.43 us -> 3.05 us
    reshape x1 -> x0, local copies, waits for them, and re-layouts: 1.46 us -> none  [body(): return applied.reshape(count, boxes_here * leaf_n)]
  transfers between devices with their start and end apart: 7 -> 0, of which waited for: 6 -> 0; matrix products, arithmetic and copies ran while one was open for 13% -> 0% of each run, Pallas kernels for 0% -> 0%
where the time goes in v1:
time: 48.4 us; the launch traced here: 48.2 us
  Pallas kernels  45.1 us (93%)
  local copies, waits for them, and re-layouts  3.05 us (6%)
    pallas_call x1, Pallas kernels, body(): pl.pallas_call(functools.partial(kernel, n_gx, n_gy, rank), out_shape=jax...  45.1 us
    unnamed x1, local copies, waits for them, and re-layouts  3.05 us

profile of v1, /device:TPU:0, one launch (start us, length us, event | category | flops | bytes accessed | tf_op | source)
XLA Modules:
  0.0 48.2 jit_solution(10152726015127375660)
XLA Ops:
  0.0 45.1 %sweep.1 = f32[16,32768]{1,0:T(8,128)} custom-call(f32[16,32768]{1,0:T(8,128)} %src.1, f32[16,96,1024]{2,1,0:T(8,128)} %bitcast.6, f32[16,1536,48]{2,1,0:T(8,128)} %bitcast.5, f32[16,96,1024]{2,1,0:T(8,128)} %bitcast.7), custom_call_target="tpu_custom_call" | custom-call | tf_op jit(solution)/shard_map/sweep/pallas_call | solution.py:288
  45.2 3.0 %copy.6 = f32[16,32768]{1,0:T(8,128)} copy(f32[16,32768]{1,0:T(8,128)} %sweep.1) | data formatting | bytes 4194304

commit v2 on v1

v2 whole, which is shorter than its diff:
```python
import functools

import jax
import jax.numpy as jnp
from jax import lax
from jax.experimental import pallas as pl
from jax.experimental.pallas import tpu as pltpu
from jax.sharding import PartitionSpec as P

F32 = jnp.float32
BF16 = jnp.bfloat16
LANES = 128
SHARES = (4, 4, 4, 4)


def parts_of(pairs):
    if sum(SHARES) != pairs:
        return [(p, 1) for p in range(pairs)]
    return [(sum(SHARES[:j]), n) for j, n in enumerate(SHARES)]


def flipped(index, bit):
    return index + bit * (1 - 2 * (lax.div(index, bit) % 2))


def crossed(index, mask):
    bit = 1
    while bit <= mask:
        if mask & bit:
            index = flipped(index, bit)
        bit *= 2
    return index


def split(value):
    high = value.astype(BF16)
    return high, (value - high.astype(F32)).astype(BF16)


def stacked(value):
    high, low = split(value)
    return jnp.concatenate(
        [
            jnp.concatenate([high, high], 1),
            jnp.concatenate([low, jnp.zeros_like(low)], 1),
        ],
        0,
    )


def across(left, right):
    return lax.dot_general(left, right, (((1,), (1,)), ((), ())), preferred_element_type=F32)


def kernel(
    n_gx, n_gy, rank,
    src, leaf, blocks, basis, out,
    src_v, leaf_v, raw, tiles, state, far, held, moved, wide,
    src_sem, leaf_sem, raw_sem, basis_sem, send_sem, recv_sem, out_sem, in_sem,
):
    pairs = leaf.shape[0]
    count = src.shape[0]
    points = leaf.shape[2]
    levels = blocks.shape[0] // 2
    parts = parts_of(pairs)
    both = 2 * rank
    pitch = raw.shape[2]
    gx, gy = lax.axis_index("gx"), lax.axis_index("gy")
    lane = lax.broadcasted_iota(jnp.int32, (count, both), 1)
    first_box = lane < rank

    def partner(level):
        bit = 2 ** (level - 1)
        if bit < n_gy:
            return gx, flipped(gy, bit)
        return flipped(gx, bit // n_gy), gy

    def src_copy(j):
        first, n = parts[j]
        here = pl.ds(first * 2 * points, n * 2 * points)
        return pltpu.make_async_copy(src.at[:, here], src_v.at[:, here], src_sem.at[j])

    def leaf_copy(j):
        here = pl.ds(*parts[j])
        return pltpu.make_async_copy(leaf.at[here], leaf_v.at[here], leaf_sem.at[j])

    def basis_copy(j):
        here = pl.ds(*parts[j])
        return pltpu.make_async_copy(basis.at[here], leaf_v.at[here], basis_sem.at[j])

    def raw_copy(i):
        return pltpu.make_async_copy(
            blocks.at[i], raw.at[i, :, pl.ds(0, 2 * pairs), :], raw_sem.at[i]
        )

    def exchange(level, j):
        here = pl.ds(*parts[j])
        return pltpu.make_async_remote_copy(
            src_ref=state.at[level, here],
            dst_ref=far.at[level, here],
            send_sem=send_sem.at[level, j],
            recv_sem=recv_sem.at[level, j],
            device_id=partner(level),
            device_id_type=pl.DeviceIdType.MESH,
        )

    def handover(b):
        return pltpu.make_async_remote_copy(
            src_ref=state.at[levels, b],
            dst_ref=moved.at[gy],
            send_sem=out_sem.at[b],
            recv_sem=in_sem.at[gy],
            device_id=(gx, b),
            device_id_type=pl.DeviceIdType.MESH,
        )

    def arrival(a):
        return pltpu.make_async_remote_copy(
            src_ref=state.at[levels, a],
            dst_ref=moved.at[a],
            send_sem=out_sem.at[a],
            recv_sem=in_sem.at[a],
            device_id=(gx, a),
            device_id_type=pl.DeviceIdType.MESH,
        )

    barrier = pltpu.get_barrier_semaphore()
    for level in range(1, levels):
        pl.semaphore_signal(barrier, inc=1, device_id=partner(level), device_id_type=pl.DeviceIdType.MESH)

    def load(j):
        src_copy(j).start()
        leaf_copy(j).start()

    load(0)
    raw_copy(0).start()
    raw_copy(1).start()
    load(1)

    def blank(i, carry):
        state[i] = jnp.zeros_like(state[i])
        return carry

    lax.fori_loop(0, levels + 1, blank, 0)

    def lay(level, which, p):
        gap = jnp.zeros((rank, LANES - rank), F32)

        def rows_of(i, c):
            rows = raw.at[i].reshape(rank * pitch, rank)
            own = rows[pl.ds(2 * p + c, rank, stride=pitch), :]
            return jnp.concatenate([own, gap], 1)

        for c in range(2):
            full = rows_of(2 * level + which, c)
            if c:
                full = pltpu.roll(full, rank, 1)
            if level == 0:
                other = rows_of(1, c)
                full += other if c else pltpu.roll(other, rank, 1)
            high, low = split(full)
            tiles[level, which, p, c * rank : (c + 1) * rank, :LANES] = high
            tiles[level, which, p, c * rank : (c + 1) * rank, LANES:] = low

    def lay_level(level):
        def step(i, carry):
            for q in range(2):
                for which in range(1 if level == 0 else 2):
                    lay(level, which, 2 * i + q)
            return carry

        raw_copy(2 * level).wait()
        raw_copy(2 * level + 1).wait()
        lax.fori_loop(0, pairs // 2, step, 0)

    def compress(p):
        high, low = split(leaf_v[p])
        h0, l0 = split(src_v[:, 2 * p * points : (2 * p + 1) * points])
        h1, l1 = split(src_v[:, (2 * p + 1) * points : (2 * p + 2) * points])
        main = across(jnp.concatenate([h0, h1, l0, l1], 0), high)
        rest = across(jnp.concatenate([h0, h1], 0), low)
        total = main[: 2 * count] + main[2 * count :] + rest
        state[0, p, :, :both] = jnp.where(first_box, total[:count], total[count:])

    def pair_up(p):
        product = across(stacked(state[0, p]), tiles[0, 0, p])
        state[1, p, :, :both] = product[:count] + product[count:]

    def own_term(level):
        def step(i, carry):
            for q in range(8):
                p = 8 * i + q
                product = across(stacked(state[level, p]), tiles[level, 0, p])
                held[p, :, :both] = product[:count] + product[count:]
            return carry

        lax.fori_loop(0, pairs // 8, step, 0)

    def combine(level, p):
        product = across(stacked(far[level, p]), tiles[level, 1, p])
        state[level + 1, p, :, :both] = held[p, :, :both] + (product[:count] + product[count:])

    def members(j):
        first, n = parts[j]
        return range(first, first + n)

    for j in range(len(parts)):
        src_copy(j).wait()
        leaf_copy(j).wait()
        if j + 2 < len(parts):
            load(j + 2)
        if j == 1:
            raw_copy(0).wait()
            raw_copy(1).wait()
        for p in members(j):
            compress(p)
        if j:
            for p in members(j - 1):
                lay(0, 0, p)
            for p in members(j - 1):
                pair_up(p)
            if j == 1:
                pl.semaphore_wait(barrier, levels - 1)
            exchange(1, j - 1).start()
    last = len(parts) - 1
    for p in members(last):
        lay(0, 0, p)
    for p in members(last):
        pair_up(p)
    exchange(1, last).start()
    for i in range(2, 2 * levels):
        raw_copy(i).start()
    for j in range(len(parts)):
        basis_copy(j).start()
    lay_level(1)
    own_term(1)
    lay_level(2)
    ahead = {1: (3,), 2: (4,), 3: (5, 6), 4: (), 5: (7,)}

    for level in range(1, levels):
        for j in range(len(parts)):
            exchange(level, j).wait_recv()
            for p in members(j):
                combine(level, p)
            if level + 1 < levels:
                exchange(level + 1, j).start()
            else:
                for p in members(j):

                    @pl.when(p != gy)
                    def _(p=p):
                        handover(p).start()

        if level + 1 < levels:
            own_term(level + 1)
        for later in ahead.get(level, ()):
            if later < levels:
                lay_level(later)
        if level == 1:
            for j in range(len(parts)):
                basis_copy(j).wait()

            def spread(p, carry):
                high, low = split(leaf_v[p])
                wide[p, :both] = high
                wide[p, both:] = low
                return carry

            lax.fori_loop(0, pairs, spread, 0)

    moved[gy] = state[levels, gy]

    def expand(a):
        high, low = split(moved[a][:, :both])
        none = jnp.zeros_like(high)
        rows = []
        for mine in (first_box, jnp.logical_not(first_box)):
            kept = jnp.where(mine, high, none)
            rows.append(jnp.concatenate([kept, kept], 1))
            rows.append(jnp.concatenate([jnp.where(mine, low, none), none], 1))
        product = jnp.dot(jnp.concatenate(rows, 0), wide[a], preferred_element_type=F32)
        for c in range(2):
            at = pl.multiple_of((2 * a + c) * points, points)
            out[:, pl.ds(at, points)] = (
                product[2 * c * count : (2 * c + 1) * count]
                + product[(2 * c + 1) * count : (2 * c + 2) * count]
            )

    hops = [0, 1, 2, 1]
    for far_off in range(5):
        ring = [d for d in range(n_gy) if hops[d % 4] + hops[d // 4 % 4] == far_off]
        sources = [crossed(gy, d) for d in ring]
        if far_off:
            for a in sources:
                arrival(a).wait_recv()
        for a in sources:
            expand(a)

    for level in range(1, levels):
        for j in range(len(parts)):
            exchange(level, j).wait_send()

    def drain(b, carry):
        @pl.when(b != gy)
        def _():
            handover(b).wait_send()

        return carry

    lax.fori_loop(0, n_gy, drain, 0)


def body(n_gx, n_gy, sources, leaf_basis, level_blocks, out_basis):
    boxes, rank, points = leaf_basis.shape
    count = sources.shape[0]
    levels = level_blocks.shape[0]
    pairs = boxes // 2
    parts = len(parts_of(pairs))
    leaf = leaf_basis.reshape(pairs, 2 * rank, points)
    basis = out_basis.reshape(pairs, 2 * rank, points)
    blocks = level_blocks.transpose(0, 1, 2, 4, 3).reshape(2 * levels, rank, boxes, rank)
    dma = pltpu.SemaphoreType.DMA
    anywhere = pl.BlockSpec(memory_space=pl.ANY)
    return pl.pallas_call(
        functools.partial(kernel, n_gx, n_gy, rank),
        out_shape=pltpu.VMEM((count, boxes * points), F32),
        in_specs=[anywhere] * 4,
        out_specs=pl.BlockSpec(memory_space=pltpu.VMEM),
        scratch_shapes=[
            pltpu.VMEM((count, boxes * points), F32),
            pltpu.VMEM((pairs, 2 * rank, points), F32),
            pltpu.VMEM((2 * levels, rank, boxes + 8, rank), F32),
            pltpu.VMEM((levels, 2, pairs, 2 * rank, 2 * LANES), BF16),
            pltpu.VMEM((levels + 1, pairs, count, LANES), F32),
            pltpu.VMEM((levels, pairs, count, LANES), F32),
            pltpu.VMEM((pairs, count, LANES), F32),
            pltpu.VMEM((n_gy, count, LANES), F32),
            pltpu.VMEM((pairs, 4 * rank, points), BF16),
            dma((parts,)),
            dma((parts,)),
            dma((2 * levels,)),
            dma((parts,)),
            dma((levels, parts)),
            dma((levels, parts)),
            dma((n_gy,)),
            dma((n_gy,)),
        ],
        compiler_params=pltpu.CompilerParams(
            collective_id=0, has_side_effects=True, vmem_limit_bytes=60 * 2**20
        ),
        name="sweep",
    )(sources, leaf, blocks, basis)


def solution(mesh):
    placed = (
        P(None, ("gx", "gy")),
        P(("gx", "gy"), None, None),
        P(None, None, None, None, ("gx", "gy")),
        P(("gx", "gy"), None, None),
    )
    return jax.shard_map(
        functools.partial(body, mesh.shape["gx"], mesh.shape["gy"]),
        mesh=mesh, in_specs=placed, out_specs=P(None, ("gx", "gy")), check_vma=False,
    )
```

time: 48.4 us -> 42.9 us (0.89)
  Pallas kernels: 45.1 us -> 41.5 us
  local copies, waits for them, and re-layouts: 3.05 us -> 1.32 us
    pallas_call x1, Pallas kernels: 45.1 us -> 41.5 us  [body(): pl.pallas_call(functools.partial(kernel, n_gx, n_gy, rank), out_shape=plt...]
    unnamed x1, local copies, waits for them, and re-layouts: 3.05 us -> 1.32 us
where the time goes in v2:
time: 42.9 us; the launch traced here: 42.8 us
  Pallas kernels  41.5 us (97%)
  local copies, waits for them, and re-layouts  1.32 us (3%)
    pallas_call x1, Pallas kernels, body(): pl.pallas_call(functools.partial(kernel, n_gx, n_gy, rank), out_shape=plt...  41.5 us
    unnamed x1, local copies, waits for them, and re-layouts  1.32 us

profile of v2, /device:TPU:0, one launch (start us, length us, event | category | flops | bytes accessed | tf_op | source)
XLA Modules:
  0.0 42.8 jit_solution(9324567563026779469)
XLA Ops:
  0.0 41.5 %sweep.1 = f32[16,32768]{1,0:T(8,128)S(1)} custom-call(f32[16,32768]{1,0:T(8,128)} %src.1, f32[16,96,1024]{2,1,0:T(8,128)} %bitcast.6, f32[16,48,32,48]{3,2,1,0:T(8,128)} %bitcast.5, f32[16,96,1024]{2,1,0:T(8,128)} %bitcast.7), custom_call_target="tpu_custom_call" | custom-call | tf_op jit(solution)/shard_map/sweep/pallas_call | solution.py:324
  41.5 1.3 %copy.6 = f32[16,32768]{1,0:T(8,128)} copy(f32[16,32768]{1,0:T(8,128)S(1)} %sweep.1) | data formatting | bytes 4194304

commit v3 on v2

--- a/solution.py
+++ b/solution.py
@@ -10,13 +10,16 @@
 F32 = jnp.float32
 BF16 = jnp.bfloat16
 LANES = 128
-SHARES = (4, 4, 4, 4)
-
-
-def parts_of(pairs):
-    if sum(SHARES) != pairs:
+SHARES = (4, 3, 3, 3, 3)
+LOADS = (1, 1, 2, 2, 2, 2, 2, 2, 2)
+AHEAD = 4
+DONE = 2
+
+
+def parts_of(pairs, shares):
+    if sum(shares) != pairs:
         return [(p, 1) for p in range(pairs)]
-    return [(sum(SHARES[:j]), n) for j, n in enumerate(SHARES)]
+    return [(sum(shares[:j]), n) for j, n in enumerate(shares)]
 
 
 def flipped(index, bit):
@@ -52,17 +55,66 @@
     return lax.dot_general(left, right, (((1,), (1,)), ((), ())), preferred_element_type=F32)
 
 
+HOPS = (0, 1, 2, 1)
+
+
+def at_distance(gy, n_gy, low, high):
+    away = [HOPS[d % 4] + HOPS[d // 4 % 4] for d in range(n_gy)]
+    near = sorted((away[d], d) for d in range(n_gy) if low <= away[d] <= high)
+    return [crossed(gy, d) for _, d in near]
+
+
+def expanded(arrived, factors, rank):
+    count = arrived.shape[0]
+    both = 2 * rank
+    first_box = lax.broadcasted_iota(jnp.int32, (count, both), 1) < rank
+    high, low = split(arrived[:, :both])
+    none = jnp.zeros_like(high)
+    rows = []
+    for mine in (first_box, jnp.logical_not(first_box)):
+        kept = jnp.where(mine, high, none)
+        rows.append(jnp.concatenate([kept, kept], 1))
+        rows.append(jnp.concatenate([jnp.where(mine, low, none), none], 1))
+    product = jnp.dot(jnp.concatenate(rows, 0), factors, preferred_element_type=F32)
+    return [
+        product[2 * c * count : (2 * c + 1) * count] + product[(2 * c + 1) * count : (2 * c + 2) * count]
+        for c in range(2)
+    ]
+
+
+def finish(n_gy, rank, part, moved, wide, out, rest, part_sem, rest_sem):
+    gy = lax.axis_index("gy")
+    points = wide.shape[2]
+
+    def place(a):
+        return pl.ds(pl.multiple_of(a * 2 * points, 2 * points), 2 * points)
+
+    copies = []
+    for i, a in enumerate(at_distance(gy, n_gy, 0, DONE)):
+        copies.append(pltpu.make_async_copy(part.at[:, place(a)], out.at[:, place(a)], part_sem.at[i]))
+        copies[-1].start()
+    for i, a in enumerate(at_distance(gy, n_gy, DONE + 1, 4)):
+        boxes = expanded(moved[a], wide[a], rank)
+        for c in range(2):
+            rest[i, :, c * points : (c + 1) * points] = boxes[c]
+        copies.append(pltpu.make_async_copy(rest.at[i], out.at[:, place(a)], rest_sem.at[i]))
+        copies[-1].start()
+    for copy in copies:
+        copy.wait()
+
+
 def kernel(
     n_gx, n_gy, rank,
-    src, leaf, blocks, basis, out,
-    src_v, leaf_v, raw, tiles, state, far, held, moved, wide,
+    src, leaf, blocks, basis, out, moved, wide,
+    src_v, leaf_v, raw, tiles, state, far, held,
     src_sem, leaf_sem, raw_sem, basis_sem, send_sem, recv_sem, out_sem, in_sem,
 ):
     pairs = leaf.shape[0]
     count = src.shape[0]
     points = leaf.shape[2]
     levels = blocks.shape[0] // 2
-    parts = parts_of(pairs)
+    parts = parts_of(pairs, SHARES)
+    loads = parts_of(pairs, LOADS)
     both = 2 * rank
     pitch = raw.shape[2]
     gx, gy = lax.axis_index("gx"), lax.axis_index("gy")
@@ -75,14 +127,14 @@
             return gx, flipped(gy, bit)
         return flipped(gx, bit // n_gy), gy
 
-    def src_copy(j):
-        first, n = parts[j]
+    def src_copy(i):
+        first, n = loads[i]
         here = pl.ds(first * 2 * points, n * 2 * points)
-        return pltpu.make_async_copy(src.at[:, here], src_v.at[:, here], src_sem.at[j])
-
-    def leaf_copy(j):
-        here = pl.ds(*parts[j])
-        return pltpu.make_async_copy(leaf.at[here], leaf_v.at[here], leaf_sem.at[j])
+        return pltpu.make_async_copy(src.at[:, here], src_v.at[:, here], src_sem.at[i])
+
+    def leaf_copy(i):
+        here = pl.ds(*loads[i])
+        return pltpu.make_async_copy(leaf.at[here], leaf_v.at[here], leaf_sem.at[i])
 
     def basis_copy(j):
         here = pl.ds(*parts[j])
@@ -128,14 +180,16 @@
     for level in range(1, levels):
         pl.semaphore_signal(barrier, inc=1, device_id=partner(level), device_id_type=pl.DeviceIdType.MESH)
 
-    def load(j):
-        src_copy(j).start()
-        leaf_copy(j).start()
-
-    load(0)
-    raw_copy(0).start()
-    raw_copy(1).start()
-    load(1)
+    def load(i):
+        src_copy(i).start()
+        leaf_copy(i).start()
+
+    def fetch(level):
+        raw_copy(2 * level).start()
+        raw_copy(2 * level + 1).start()
+
+    for i in range(min(AHEAD, len(loads))):
+        load(i)
 
     def blank(i, carry):
         state[i] = jnp.zeros_like(state[i])
@@ -171,6 +225,8 @@
 
         raw_copy(2 * level).wait()
         raw_copy(2 * level + 1).wait()
+        if level + 2 < levels:
+            fetch(level + 2)
         lax.fori_loop(0, pairs // 2, step, 0)
 
     def compress(p):
@@ -204,37 +260,48 @@
         first, n = parts[j]
         return range(first, first + n)
 
+    last = len(parts) - 1
+    next_load = 0
     for j in range(len(parts)):
-        src_copy(j).wait()
-        leaf_copy(j).wait()
-        if j + 2 < len(parts):
-            load(j + 2)
         if j == 1:
             raw_copy(0).wait()
             raw_copy(1).wait()
-        for p in members(j):
-            compress(p)
+        while next_load < len(loads) and loads[next_load][0] < sum(parts[j]):
+            src_copy(next_load).wait()
+            leaf_copy(next_load).wait()
+            if next_load == 0:
+                fetch(0)
+            if next_load + AHEAD < len(loads):
+                load(next_load + AHEAD)
+            elif next_load + AHEAD == len(loads):
+                fetch(1)
+            elif next_load + AHEAD == len(loads) + 1:
+                fetch(2)
+            if j == 0:
+                for p in range(loads[next_load][0], sum(loads[next_load])):
+                    compress(p)
+            next_load += 1
         if j:
+            for p in members(j):
+                compress(p)
             for p in members(j - 1):
                 lay(0, 0, p)
+            if j == last:
+                for p in members(last):
+                    lay(0, 0, p)
             for p in members(j - 1):
                 pair_up(p)
             if j == 1:
                 pl.semaphore_wait(barrier, levels - 1)
             exchange(1, j - 1).start()
-    last = len(parts) - 1
-    for p in members(last):
-        lay(0, 0, p)
     for p in members(last):
         pair_up(p)
     exchange(1, last).start()
-    for i in range(2, 2 * levels):
-        raw_copy(i).start()
-    for j in range(len(parts)):
-        basis_copy(j).start()
     lay_level(1)
     own_term(1)
     lay_level(2)
+    for j in range(len(parts)):
+        basis_copy(j).start()
     ahead = {1: (3,), 2: (4,), 3: (5, 6), 4: (), 5: (7,)}
 
     for level in range(1, levels):
@@ -256,7 +323,7 @@
         for later in ahead.get(level, ()):
             if later < levels:
                 lay_level(later)
-        if level == 1:
+        if level == 3:
             for j in range(len(parts)):
                 basis_copy(j).wait()
 
@@ -270,31 +337,17 @@
 
     moved[gy] = state[levels, gy]
 
-    def expand(a):
-        high, low = split(moved[a][:, :both])
-        none = jnp.zeros_like(high)
-        rows = []
-        for mine in (first_box, jnp.logical_not(first_box)):
-            kept = jnp.where(mine, high, none)
-            rows.append(jnp.concatenate([kept, kept], 1))
-            rows.append(jnp.concatenate([jnp.where(mine, low, none), none], 1))
-        product = jnp.dot(jnp.concatenate(rows, 0), wide[a], preferred_element_type=F32)
-        for c in range(2):
-            at = pl.multiple_of((2 * a + c) * points, points)
-            out[:, pl.ds(at, points)] = (
-                product[2 * c * count : (2 * c + 1) * count]
-                + product[(2 * c + 1) * count : (2 * c + 2) * count]
-            )
-
-    hops = [0, 1, 2, 1]
-    for far_off in range(5):
-        ring = [d for d in range(n_gy) if hops[d % 4] + hops[d // 4 % 4] == far_off]
-        sources = [crossed(gy, d) for d in ring]
-        if far_off:
-            for a in sources:
+    for hops in range(5):
+        ring = at_distance(gy, n_gy, hops, hops)
+        if hops:
+            for a in ring:
                 arrival(a).wait_recv()
-        for a in sources:
-            expand(a)
+        if hops <= DONE:
+            for a in ring:
+                outputs = expanded(moved[a], wide[a], rank)
+                for c in range(2):
+                    at = pl.multiple_of((2 * a + c) * points, points)
+                    out[:, pl.ds(at, points)] = outputs[c]
 
     for level in range(1, levels):
         for j in range(len(parts)):
@@ -315,17 +368,23 @@
     count = sources.shape[0]
     levels = level_blocks.shape[0]
     pairs = boxes // 2
-    parts = len(parts_of(pairs))
+    parts = len(parts_of(pairs, SHARES))
+    loads = len(parts_of(pairs, LOADS))
     leaf = leaf_basis.reshape(pairs, 2 * rank, points)
     basis = out_basis.reshape(pairs, 2 * rank, points)
     blocks = level_blocks.transpose(0, 1, 2, 4, 3).reshape(2 * levels, rank, boxes, rank)
     dma = pltpu.SemaphoreType.DMA
     anywhere = pl.BlockSpec(memory_space=pl.ANY)
-    return pl.pallas_call(
+    held = pl.BlockSpec(memory_space=pltpu.VMEM)
+    part, moved, wide = pl.pallas_call(
         functools.partial(kernel, n_gx, n_gy, rank),
-        out_shape=pltpu.VMEM((count, boxes * points), F32),
+        out_shape=(
+            pltpu.VMEM((count, boxes * points), F32),
+            pltpu.VMEM((n_gy, count, LANES), F32),
+            pltpu.VMEM((pairs, 4 * rank, points), BF16),
+        ),
         in_specs=[anywhere] * 4,
-        out_specs=pl.BlockSpec(memory_space=pltpu.VMEM),
+        out_specs=(held,) * 3,
         scratch_shapes=[
             pltpu.VMEM((count, boxes * points), F32),
             pltpu.VMEM((pairs, 2 * rank, points), F32),
@@ -334,10 +393,8 @@
             pltpu.VMEM((levels + 1, pairs, count, LANES), F32),
             pltpu.VMEM((levels, pairs, count, LANES), F32),
             pltpu.VMEM((pairs, count, LANES), F32),
-            pltpu.VMEM((n_gy, count, LANES), F32),
-            pltpu.VMEM((pairs, 4 * rank, points), BF16),
-            dma((parts,)),
-            dma((parts,)),
+            dma((loads,)),
+            dma((loads,)),
             dma((2 * levels,)),
             dma((parts,)),
             dma((levels, parts)),
@@ -346,10 +403,24 @@
             dma((n_gy,)),
         ],
         compiler_params=pltpu.CompilerParams(
-            collective_id=0, has_side_effects=True, vmem_limit_bytes=60 * 2**20
+            collective_id=0, has_side_effects=True, vmem_limit_bytes=46 * 2**20
         ),
         name="sweep",
     )(sources, leaf, blocks, basis)
+    late = sum(HOPS[d % 4] + HOPS[d // 4 % 4] > DONE for d in range(n_gy))
+    return pl.pallas_call(
+        functools.partial(finish, n_gy, rank),
+        out_shape=jax.ShapeDtypeStruct((count, boxes * points), F32),
+        in_specs=[held] * 3,
+        out_specs=anywhere,
+        scratch_shapes=[
+            pltpu.VMEM((max(late, 1), count, 2 * points), F32),
+            dma((n_gy - late,)),
+            dma((max(late, 1),)),
+        ],
+        compiler_params=pltpu.CompilerParams(vmem_limit_bytes=8 * 2**20),
+        name="finish",
+    )(part, moved, wide)
 
 
 def solution(mesh):

time: 42.9 us -> 41.6 us (0.970)
  local copies, waits for them, and re-layouts: 1.32 us -> 0 us
    unnamed x1 -> x0, local copies, waits for them, and re-layouts: 1.32 us -> none
    pallas_call x1 -> x2, Pallas kernels: 41.5 us -> 41.5 us  [the longest x1 39.9 us: body(): pl.pallas_call(functools.partial(kernel, n_gx, n_gy, rank), out_shape=(pl...]
where the time goes in v3:
time: 41.6 us; the launch traced here: 41.5 us
  Pallas kernels  41.5 us (100%)
    pallas_call x1, Pallas kernels, body(): pl.pallas_call(functools.partial(kernel, n_gx, n_gy, rank), out_shape=(pl...  39.9 us
    pallas_call x1, Pallas kernels, body(): pl.pallas_call(functools.partial(finish, n_gy, rank), out_shape=jax.Shape...  1.63 us

profile of v3, /device:TPU:0, one launch (start us, length us, event | category | flops | bytes accessed | tf_op | source)
XLA Modules:
  0.0 41.5 jit_solution(11362057422616110423)
XLA Ops:
  0.0 39.9 %sweep.1 = (f32[16,32768]{1,0:T(8,128)S(1)}, f32[16,16,128]{2,1,0:T(8,128)S(1)}, bf16[16,192,1024]{2,1,0:T(8,128)(2,1)S(1)}) custom-call(f32[16,32768]{1,0:T(8,128)} %src.1, f32[16,96,1024]{2,1,0:T(8,128)} %bitcast.6, f32[16,48,32,48]{3,2,1,0:T(8,128)} %bitcast.5, f32[16,96,1024]{2,1,0:T(8,128)} %bitcast.7), custom_call_target="tpu_custom_call" | custom-call | tf_op jit(solution)/shard_map/sweep/pallas_call | solution.py:379
  39.9 1.6 %finish.1 = f32[16,32768]{1,0:T(8,128)} custom-call(f32[16,32768]{1,0:T(8,128)S(1)} %get-tuple-element.8.part, f32[16,16,128]{2,1,0:T(8,128)S(1)} %get-tuple-element.9.moved, bf16[16,192,1024]{2,1,0:T(8,128)(2,1)S(1)} %get-tuple-element.10.wide), custom_call_target="tpu_custom_call" | custom-call | tf_op jit(solution)/shard_map/finish/pallas_call | solution.py:411

commit v4 on v3

--- a/solution.py
+++ b/solution.py
@@ -10,10 +10,11 @@
 F32 = jnp.float32
 BF16 = jnp.bfloat16
 LANES = 128
-SHARES = (4, 3, 3, 3, 3)
+SHARES = (3, 4, 3, 3, 3)
 LOADS = (1, 1, 2, 2, 2, 2, 2, 2, 2)
 AHEAD = 4
 DONE = 2
+NEAR = 3
 
 
 def parts_of(pairs, shares):
@@ -255,6 +256,11 @@
     def combine(level, p):
         product = across(stacked(far[level, p]), tiles[level, 1, p])
         state[level + 1, p, :, :both] = held[p, :, :both] + (product[:count] + product[count:])
+
+    def combine_both(level, p):
+        product = across(stacked(state[level, p]), tiles[level, 0, p])
+        product += across(stacked(far[level, p]), tiles[level, 1, p])
+        state[level + 1, p, :, :both] = product[:count] + product[count:]
 
     def members(j):
         first, n = parts[j]
@@ -299,31 +305,42 @@
     exchange(1, last).start()
     lay_level(1)
     own_term(1)
-    lay_level(2)
     for j in range(len(parts)):
         basis_copy(j).start()
     ahead = {1: (3,), 2: (4,), 3: (5, 6), 4: (), 5: (7,)}
 
+    near = 1 + (n_gy.bit_length() - 1)
     for level in range(1, levels):
-        for j in range(len(parts)):
-            exchange(level, j).wait_recv()
-            for p in members(j):
-                combine(level, p)
-            if level + 1 < levels:
-                exchange(level + 1, j).start()
-            else:
+        groups = [[j] for j in range(len(parts))]
+        if level == near:
+            groups = [range(NEAR), range(NEAR, len(parts))]
+        for group in groups:
+            for j in group:
+                exchange(level, j).wait_recv()
+            for j in group:
                 for p in members(j):
-
-                    @pl.when(p != gy)
-                    def _(p=p):
-                        handover(p).start()
-
-        if level + 1 < levels:
+                    if level == near:
+                        combine_both(level, p)
+                    else:
+                        combine(level, p)
+            for j in group:
+                if level + 1 < levels:
+                    exchange(level + 1, j).start()
+                else:
+                    for p in members(j):
+
+                        @pl.when(p != gy)
+                        def _(p=p):
+                            handover(p).start()
+
+        if level == 1:
+            lay_level(2)
+        if level + 1 < levels and level + 1 != near:
             own_term(level + 1)
         for later in ahead.get(level, ()):
             if later < levels:
                 lay_level(later)
-        if level == 3:
+        if level == levels - 2:
             for j in range(len(parts)):
                 basis_copy(j).wait()
 

time: 41.6 us -> 40.4 us (0.971)
  Pallas kernels: 41.5 us -> 40.2 us
    pallas_call x1, Pallas kernels: 39.9 us -> 38.6 us  [body(): pl.pallas_call(functools.partial(kernel, n_gx, n_gy, rank), out_shape=(pl...]
where the time goes in v4:
time: 40.4 us; the launch traced here: 40.3 us
  Pallas kernels  40.2 us (100%)
    pallas_call x1, Pallas kernels, body(): pl.pallas_call(functools.partial(kernel, n_gx, n_gy, rank), out_shape=(pl...  38.6 us
    pallas_call x1, Pallas kernels, body(): pl.pallas_call(functools.partial(finish, n_gy, rank), out_shape=jax.Shape...  1.63 us

profile of v4, /device:TPU:0, one launch (start us, length us, event | category | flops | bytes accessed | tf_op | source)
XLA Modules:
  0.0 40.3 jit_solution(12286049151207712298)
XLA Ops:
  0.0 38.6 %sweep.1 = (f32[16,32768]{1,0:T(8,128)S(1)}, f32[16,16,128]{2,1,0:T(8,128)S(1)}, bf16[16,192,1024]{2,1,0:T(8,128)(2,1)S(1)}) custom-call(f32[16,32768]{1,0:T(8,128)} %src.1, f32[16,96,1024]{2,1,0:T(8,128)} %bitcast.6, f32[16,48,32,48]{3,2,1,0:T(8,128)} %bitcast.5, f32[16,96,1024]{2,1,0:T(8,128)} %bitcast.7), custom_call_target="tpu_custom_call" | custom-call | tf_op jit(solution)/shard_map/sweep/pallas_call | solution.py:396
  38.6 1.6 %finish.1 = f32[16,32768]{1,0:T(8,128)} custom-call(f32[16,32768]{1,0:T(8,128)S(1)} %get-tuple-element.8.part, f32[16,16,128]{2,1,0:T(8,128)S(1)} %get-tuple-element.9.moved, bf16[16,192,1024]{2,1,0:T(8,128)(2,1)S(1)} %get-tuple-element.10.wide), custom_call_target="tpu_custom_call" | custom-call | tf_op jit(solution)/shard_map/finish/pallas_call | solution.py:428
